TPU v7x, 512 devices: a whole 4x8x8 slice. The times are simulated.
512 devices in a mesh: tm: 128 (over z, y, core), swath: 4 (over x).
Axes of the slice: x: 4, y: 8, z: 8, core: 2. Of those that a mesh axis runs over, the one named last changes fastest.
Arguments:
- design: bfloat16 [128, 2048, 512], P('tm', 'swath'), may hold values from -6 to 6
- process: bfloat16 [128, 512, 512], P('tm', 'swath')
- prior_prec: float32 [128, 512], P('tm', 'swath'), may hold values from 0.05 to 0.5
- routes: int32 [128, 16], P('tm', 'swath'), may hold values from -1 to 127, as said below
- counts: int32 [128, 4], P('tm', 'swath'), may hold values from 1 to 4
Outputs:
- reduced_diag: float32 [128, 512, 512], P('tm', 'swath')
- reduced_coupling: float32 [128, 512, 512], P('tm', 'swath')
Inputs may be any that keep to these rules, and one draw needn't show every extreme that they name: `routes`: each value is the holder's own time block i or i + 1, or -1 only where i + 1 would be 128; of one holder's 4 blocks, exactly 2 name i and the others i + 1 or -1.
All inputs are finite; a program needn't handle non-finite values.
Results may differ from a plain program's by a relative error of at most 0.00073.
Values may be sent and summed in bfloat16 or wider, within the bound.
No kernel may reach another device: no remote copies, remote signals or barrier semaphores. Data moves between devices by JAX's collectives and lax.ppermute only.
A program may use at most 64 MiB of HBM per device.

v0:
```python
import jax
import jax.numpy as jnp
from jax import lax
from jax.sharding import PartitionSpec as P

LEVELS = 3


def passed_along(block, axis, distance):
    devices = range(lax.axis_size(axis))
    route = [(i - distance, i) for i in devices if i - distance in devices]
    return lax.ppermute(block, axis, route)


def tri_solve(factor, right):
    return lax.linalg.triangular_solve(factor, right, left_side=True, lower=True)


def inner_rows(left_side, right_side):
    return lax.dot_general(
        left_side,
        right_side,
        (((0,), (0,)), ((), ())),
        precision=lax.Precision.HIGHEST,
        preferred_element_type=jnp.float32,
    )


def compact(scaled, wanted, slot_count):
    sort_key = jnp.where(wanted, 0, 1).astype(jnp.int32)
    picked = jnp.argsort(sort_key, stable=True)[:slot_count]
    kept = jnp.take(sort_key, picked) == 0
    return jnp.where(kept[:, None, None], scaled[picked], 0.0).astype(jnp.bfloat16)


def shards(design, process, prior_prec, routes, counts):
    row_count = process.shape[1]
    order_size = process.shape[2]
    time_count = lax.axis_size("tm")
    my_time = lax.axis_index("tm")
    swath_index = lax.axis_index("swath")
    block_count = routes.shape[1]
    slot_count = block_count // 2
    block_rows = design.shape[1] // block_count
    total_slots = 2 * slot_count * block_rows * lax.axis_size("swath")
    row_start = swath_index * row_count
    raw_rows = design[0].reshape(block_count, block_rows, order_size).astype(jnp.float32)
    mean_sq = jnp.mean(raw_rows * raw_rows, axis=-1, keepdims=True)
    scaled = raw_rows * lax.rsqrt(4.0 * total_slots * (mean_sq + 1e-06))
    live = jnp.arange(block_count) < counts[0, 0]
    target = routes[0]
    own_blocks = compact(scaled, live & (target == my_time), slot_count)
    ahead_blocks = compact(scaled, live & (target == my_time + 1), slot_count)
    incoming, previous = passed_along((ahead_blocks, process), "tm", 1)
    gram_input = jnp.concatenate([own_blocks, incoming], axis=0).reshape(-1, order_size)
    shard_rows = lax.all_gather(gram_input, "swath", axis=0, tiled=True)
    columns = lax.dynamic_slice_in_dim(shard_rows, row_start, row_count, 1)
    gram = lax.dot_general(
        columns, shard_rows, (((0,), (0,)), ((), ())), preferred_element_type=jnp.float32
    )
    unit_rows = jnp.arange(order_size)[None, :] == jnp.arange(row_count)[:, None] + row_start
    diag_rows = previous[0].astype(jnp.float32) + process[0].astype(jnp.float32) + gram
    diag_rows = diag_rows + jnp.where(unit_rows, prior_prec[0][:, None], 0.0)
    coup_rows = -process[0].astype(jnp.float32)
    unit_full = jnp.eye(order_size, dtype=jnp.float32)
    for level in range(LEVELS):
        distance = 2**level
        full_diag, full_coup = (
            lax.all_gather(diag_rows, "swath", axis=0, tiled=True),
            lax.all_gather(coup_rows, "swath", axis=0, tiled=True),
        )
        factor = jnp.linalg.cholesky(full_diag)
        solved = tri_solve(factor, full_coup)
        own_cols = lax.dynamic_slice_in_dim(solved, row_start, row_count, 1)
        eliminated = inner_rows(own_cols, solved)
        left_term = passed_along(eliminated, "tm", distance)
        far_factor, far_solved = passed_along((factor, solved), "tm", -distance)
        has_partner = my_time + distance < time_count
        far_factor = jnp.where(has_partner, far_factor, unit_full)
        cross = tri_solve(far_factor, full_coup.T)
        cross_cols = lax.dynamic_slice_in_dim(cross, row_start, row_count, 1)
        right_term = inner_rows(cross_cols, cross)
        new_coupling = inner_rows(cross_cols, far_solved)
        diag_rows = diag_rows - left_term - jnp.where(has_partner, right_term, 0.0)
        coup_rows = -new_coupling
    return (diag_rows[None], coup_rows[None])


def solution(mesh):
    return jax.shard_map(
        shards,
        mesh=mesh,
        in_specs=(
            P("tm", "swath", None),
            P("tm", "swath", None),
            P("tm", "swath"),
            P("tm", "swath"),
            P("tm", "swath"),
        ),
        out_specs=(P("tm", "swath", None), P("tm", "swath", None)),
        check_vma=False,
    )
```

profile of v0, /device:TPU:16, one launch (start us, length us, event | category | flops | bytes accessed | tf_op | source)
XLA Modules:
  0.0 882.1 jit_solution(11233047935860242572)
XLA Ops:
  17.1 4.4 collective-permute-done.1
  24.6 4.3 collective-permute-done
  28.9 35.5 %all-gather.9.cloned.1.call-done = bf16[2048,512]{1,0:T(8,128)(2,1)} async-done(((bf16[512,512]{1,0:T(8,128)(2,1)}), bf16[2048,512]{1,0:T(8,128)(2,1)}) %all-gather.9.cloned.1.call-update) | async-done | bytes 2097168 | tf_op jit(solution)/shard_map/all_gather | solution.py:56
  64.4 3.3 fusion.71
  68.6 30.6 %all-gather.11.cloned.1.call-done = f32[512,512]{0,1:T(8,128)} async-done(((f32[128,512]{0,1:T(8,128)}), f32[512,512]{0,1:T(8,128)}) %all-gather.11.cloned.1.call-update) | async-done | bytes 1048592 | tf_op jit(solution)/shard_map/all_gather | solution.py:69
  101.1 11.7 %cholesky.374 = f32[128,128]{1,0:T(8,128)S(1)} custom-call(f32[128,128]{1,0:T(8,128)S(1)} %cholesky.586), custom_call_target="Cholesky" | custom-call | tf_op jit(solution)/shard_map/jit(cholesky)/cholesky | solution.py:72
  113.0 9.8 %custom-call.34 = f32[1,128,128]{1,2,0:T(8,128)S(1)} custom-call(f32[1,128,128]{2,1,0:T(8,128)S(1)} %get-tuple-element.152), custom_call_target="InvertDiagBlocksLowerTriangular" | custom-call | tf_op jit(solution)/shard_map/jit(cholesky)/cholesky | solution.py:72
  123.5 11.7 %cholesky.393 = f32[128,128]{1,0:T(8,128)S(1)} custom-call(f32[128,128]{1,0:T(8,128)S(1)} %cholesky.590), custom_call_target="Cholesky" | custom-call | tf_op jit(solution)/shard_map/jit(cholesky)/cholesky | solution.py:72
  135.2 10.2 %custom-call.35 = f32[1,128,128]{1,2,0:T(8,128)S(1)} custom-call(f32[1,128,128]{2,1,0:T(8,128)S(1)} %get-tuple-element.149), custom_call_target="InvertDiagBlocksLowerTriangular" | custom-call | tf_op jit(solution)/shard_map/jit(cholesky)/cholesky | solution.py:72
  146.1 11.7 %cholesky.414 = f32[128,128]{1,0:T(8,128)S(1)} custom-call(f32[128,128]{1,0:T(8,128)S(1)} %cholesky.595), custom_call_target="Cholesky" | custom-call | tf_op jit(solution)/shard_map/jit(cholesky)/cholesky | solution.py:72
  157.9 9.8 %custom-call.36 = f32[1,128,128]{1,2,0:T(8,128)S(1)} custom-call(f32[1,128,128]{2,1,0:T(8,128)S(1)} %get-tuple-element.146), custom_call_target="InvertDiagBlocksLowerTriangular" | custom-call | tf_op jit(solution)/shard_map/jit(cholesky)/cholesky | solution.py:72
  168.3 11.7 %cholesky.431 = f32[128,128]{1,0:T(8,128)S(1)} custom-call(f32[128,128]{1,0:T(8,128)S(1)} %convolution_subtract_fusion.14), custom_call_target="Cholesky" | custom-call | tf_op jit(solution)/shard_map/jit(cholesky)/cholesky | solution.py:72
  185.5 7.5 while.12
  193.0 39.3 %custom-call.37 = f32[4,128,128]{1,2,0:T(8,128)S(1)} custom-call(f32[4,128,128]{2,1,0:T(8,128)S(1)} %get-tuple-element.47), custom_call_target="InvertDiagBlocksLowerTriangular" | custom-call | tf_op jit(solution)/shard_map/triangular_solve/custom-call.3 | solution.py:16
  246.1 5.0 collective-permute-done.3
  251.9 10.2 %while.13 = (s32[]{:T(128)}, f32[512,512]{1,0:T(8,128)S(1)}, s32[4,2]{0,1:T(2,128)S(1)}, f32[4,128,128]{2,1,0:T(8,128)}, s32[]{:T(128)}) while((s32[]{:T(128)}, f32[512,512]{1,0:T(8,128)S(1)}, s32[4,2]{0,1:T(2,128)S(1)}, f32[4,128,128]{2,1,0:T(8,128)}, s32[]{:T(128)}) %tuple.157), condition=%wide.while_cond.clone, body=%wide.while_body.clone.sunk | while | flops 2 | bytes 132205 | solution.py:16
  262.2 40.7 %custom-call.38 = f32[4,128,128]{1,2,0:T(8,128)} custom-call(f32[4,128,128]{2,1,0:T(8,128)} %get-tuple-element.48), custom_call_target="InvertDiagBlocksLowerTriangular" | custom-call | tf_op jit(solution)/shard_map/triangular_solve/custom-call.3 | solution.py:16
  310.6 3.8 collective-permute-start.4
  314.4 12.3 %collective-permute-done.4 = f32[512,512]{1,0:T(8,128)S(1)} collective-permute-done((f32[512,512]{1,0:T(8,128)S(1)}, f32[512,512]{1,0:T(8,128)S(1)}, u32[]{:S(2)}, u32[]{:S(2)}) %collective-permute-start.4) | collective-permute-done | bytes 1048608 | tf_op jit(solution)/shard_map/ppermute | solution.py:12
  328.6 15.1 %all-gather.13.cloned.1.call-done = f32[512,512]{0,1:T(8,128)} async-done(((f32[128,512]{0,1:T(8,128)}), f32[512,512]{0,1:T(8,128)}) %all-gather.13.cloned.1.call-update) | async-done | bytes 1048592 | tf_op jit(solution)/shard_map/all_gather | solution.py:69
  345.6 11.7 %cholesky.446 = f32[128,128]{1,0:T(8,128)S(1)} custom-call(f32[128,128]{1,0:T(8,128)S(1)} %cholesky.599), custom_call_target="Cholesky" | custom-call | tf_op jit(solution)/shard_map/jit(cholesky)/cholesky | solution.py:72
  357.5 9.8 %custom-call.39 = f32[1,128,128]{1,2,0:T(8,128)S(1)} custom-call(f32[1,128,128]{2,1,0:T(8,128)S(1)} %get-tuple-element.142), custom_call_target="InvertDiagBlocksLowerTriangular" | custom-call | tf_op jit(solution)/shard_map/jit(cholesky)/cholesky | solution.py:72
  368.0 11.7 %cholesky.465 = f32[128,128]{1,0:T(8,128)S(1)} custom-call(f32[128,128]{1,0:T(8,128)S(1)} %cholesky.603), custom_call_target="Cholesky" | custom-call | tf_op jit(solution)/shard_map/jit(cholesky)/cholesky | solution.py:72
  379.7 10.0 %custom-call.40 = f32[1,128,128]{1,2,0:T(8,128)S(1)} custom-call(f32[1,128,128]{2,1,0:T(8,128)S(1)} %get-tuple-element.139), custom_call_target="InvertDiagBlocksLowerTriangular" | custom-call | tf_op jit(solution)/shard_map/jit(cholesky)/cholesky | solution.py:72
  390.4 11.7 %cholesky.486 = f32[128,128]{1,0:T(8,128)S(1)} custom-call(f32[128,128]{1,0:T(8,128)S(1)} %cholesky.608), custom_call_target="Cholesky" | custom-call | tf_op jit(solution)/shard_map/jit(cholesky)/cholesky | solution.py:72
  402.1 9.8 %custom-call.41 = f32[1,128,128]{1,2,0:T(8,128)S(1)} custom-call(f32[1,128,128]{2,1,0:T(8,128)S(1)} %get-tuple-element.136), custom_call_target="InvertDiagBlocksLowerTriangular" | custom-call | tf_op jit(solution)/shard_map/jit(cholesky)/cholesky | solution.py:72
  412.5 11.7 %cholesky.503 = f32[128,128]{1,0:T(8,128)S(1)} custom-call(f32[128,128]{1,0:T(8,128)S(1)} %convolution_subtract_fusion.13), custom_call_target="Cholesky" | custom-call | tf_op jit(solution)/shard_map/jit(cholesky)/cholesky | solution.py:72
  429.7 7.5 while.14
  437.3 39.3 %custom-call.42 = f32[4,128,128]{1,2,0:T(8,128)S(1)} custom-call(f32[4,128,128]{2,1,0:T(8,128)S(1)} %get-tuple-element.49), custom_call_target="InvertDiagBlocksLowerTriangular" | custom-call | tf_op jit(solution)/shard_map/triangular_solve/custom-call.3 | solution.py:16
  486.9 3.8 collective-permute-start.5
  490.7 15.6 %collective-permute-done.6 = f32[512,512]{1,0:T(8,128)S(1)} collective-permute-done((f32[512,512]{1,0:T(8,128)S(1)}, f32[512,512]{1,0:T(8,128)S(1)}, u32[]{:S(2)}, u32[]{:S(2)}) %collective-permute-start.6) | collective-permute-done | bytes 1048608 | tf_op jit(solution)/shard_map/ppermute | solution.py:12
  507.1 10.2 %while.15 = (s32[]{:T(128)}, f32[512,512]{1,0:T(8,128)S(1)}, s32[4,2]{0,1:T(2,128)S(1)}, f32[4,128,128]{2,1,0:T(8,128)}, s32[]{:T(128)}) while((s32[]{:T(128)}, f32[512,512]{1,0:T(8,128)S(1)}, s32[4,2]{0,1:T(2,128)S(1)}, f32[4,128,128]{2,1,0:T(8,128)}, s32[]{:T(128)}) %tuple.159), condition=%wide.while_cond.clone.2, body=%wide.while_body.clone.2.sunk | while | flops 2 | bytes 132205 | solution.py:16
  517.3 40.7 %custom-call.43 = f32[4,128,128]{1,2,0:T(8,128)} custom-call(f32[4,128,128]{2,1,0:T(8,128)} %get-tuple-element.50), custom_call_target="InvertDiagBlocksLowerTriangular" | custom-call | tf_op jit(solution)/shard_map/triangular_solve/custom-call.3 | solution.py:16
  570.0 23.3 %collective-permute-done.7 = f32[512,512]{1,0:T(8,128)S(1)} collective-permute-done((f32[512,512]{1,0:T(8,128)S(1)}, f32[512,512]{1,0:T(8,128)S(1)}, u32[]{:S(2)}, u32[]{:S(2)}) %collective-permute-start.7) | collective-permute-done | bytes 1048608 | tf_op jit(solution)/shard_map/ppermute | solution.py:12
  594.9 4.9 all-gather.17.cloned.1.call-done
  601.6 11.7 %cholesky.518 = f32[128,128]{1,0:T(8,128)S(1)} custom-call(f32[128,128]{1,0:T(8,128)S(1)} %cholesky.612), custom_call_target="Cholesky" | custom-call | tf_op jit(solution)/shard_map/jit(cholesky)/cholesky | solution.py:72
  613.5 9.8 %custom-call.44 = f32[1,128,128]{1,2,0:T(8,128)S(1)} custom-call(f32[1,128,128]{2,1,0:T(8,128)S(1)} %get-tuple-element.132), custom_call_target="InvertDiagBlocksLowerTriangular" | custom-call | tf_op jit(solution)/shard_map/jit(cholesky)/cholesky | solution.py:72
  624.0 11.7 %cholesky.537 = f32[128,128]{1,0:T(8,128)S(1)} custom-call(f32[128,128]{1,0:T(8,128)S(1)} %cholesky.616), custom_call_target="Cholesky" | custom-call | tf_op jit(solution)/shard_map/jit(cholesky)/cholesky | solution.py:72
  635.8 10.0 %custom-call.45 = f32[1,128,128]{1,2,0:T(8,128)S(1)} custom-call(f32[1,128,128]{2,1,0:T(8,128)S(1)} %get-tuple-element.129), custom_call_target="InvertDiagBlocksLowerTriangular" | custom-call | tf_op jit(solution)/shard_map/jit(cholesky)/cholesky | solution.py:72
  646.4 11.7 %cholesky.558 = f32[128,128]{1,0:T(8,128)S(1)} custom-call(f32[128,128]{1,0:T(8,128)S(1)} %cholesky.621), custom_call_target="Cholesky" | custom-call | tf_op jit(solution)/shard_map/jit(cholesky)/cholesky | solution.py:72
  658.2 9.8 %custom-call.46 = f32[1,128,128]{1,2,0:T(8,128)S(1)} custom-call(f32[1,128,128]{2,1,0:T(8,128)S(1)} %get-tuple-element.126), custom_call_target="InvertDiagBlocksLowerTriangular" | custom-call | tf_op jit(solution)/shard_map/jit(cholesky)/cholesky | solution.py:72
  668.6 12.1 %cholesky.575 = f32[128,128]{1,0:T(8,128)S(1)} custom-call(f32[128,128]{1,0:T(8,128)S(1)} %convolution_subtract_fusion.12), custom_call_target="Cholesky" | custom-call | tf_op jit(solution)/shard_map/jit(cholesky)/cholesky | solution.py:72
  686.0 7.9 while.16
  693.9 39.3 %custom-call.47 = f32[4,128,128]{1,2,0:T(8,128)S(1)} custom-call(f32[4,128,128]{2,1,0:T(8,128)S(1)} %get-tuple-element.51), custom_call_target="InvertDiagBlocksLowerTriangular" | custom-call | tf_op jit(solution)/shard_map/triangular_solve/custom-call.3 | solution.py:16
  745.4 6.2 collective-permute-start.8
  751.6 59.3 %collective-permute-done.9 = f32[512,512]{1,0:T(8,128)S(1)} collective-permute-done((f32[512,512]{1,0:T(8,128)S(1)}, f32[512,512]{1,0:T(8,128)S(1)}, u32[]{:S(2)}, u32[]{:S(2)}) %collective-permute-start.9) | collective-permute-done | bytes 1048608 | tf_op jit(solution)/shard_map/ppermute | solution.py:12
  811.8 10.4 %while.17 = (s32[]{:T(128)}, f32[512,512]{1,0:T(8,128)S(1)}, s32[4,2]{0,1:T(2,128)S(1)}, f32[4,128,128]{2,1,0:T(8,128)}, s32[]{:T(128)}) while((s32[]{:T(128)}, f32[512,512]{1,0:T(8,128)S(1)}, s32[4,2]{0,1:T(2,128)S(1)}, f32[4,128,128]{2,1,0:T(8,128)}, s32[]{:T(128)}) %tuple.161), condition=%wide.while_cond.clone.4, body=%wide.while_body.clone.4.sunk | while | flops 2 | bytes 132205 | solution.py:16
  822.2 40.7 %custom-call.48 = f32[4,128,128]{1,2,0:T(8,128)} custom-call(f32[4,128,128]{2,1,0:T(8,128)} %get-tuple-element.52), custom_call_target="InvertDiagBlocksLowerTriangular" | custom-call | tf_op jit(solution)/shard_map/triangular_solve/custom-call.3 | solution.py:16
  (284 shorter events, 160.8 us)
Async XLA Ops:
  7.2 57.3 %all-gather.9.cloned.1.call-start = ((), (), s32[]{:S(2)}) async-start(), calls=%async_computation | async-start | bytes 2621440 | tf_op jit(solution)/shard_map/all_gather | solution.py:56
  13.1 9.3 %copy-start.12 = (bf16[1,128,512]{2,1,0:T(8,128)(2,1)S(1)}, bf16[1,128,512]{2,1,0:T(8,128)(2,1)}, u32[]{:S(2)}) copy-start(bf16[1,128,512]{2,1,0:T(8,128)(2,1)} %param.11) | copy-start | bytes 393220
  13.7 50.7 %copy-start.13 = (f32[1,128]{1,0:T(1,128)S(1)}, f32[1,128]{1,0:T(1,128)}, u32[]{:S(2)}) copy-start(f32[1,128]{1,0:T(1,128)} %param.12) | copy-start | bytes 1540
  13.9 7.7 collective-permute-start.1
  22.4 76.8 %all-gather.11.cloned.1.call-start = ((), (), s32[]{:S(2)}) async-start(), calls=%async_computation.1 | async-start | bytes 1310720 | tf_op jit(solution)/shard_map/all_gather | solution.py:69
  22.6 6.3 collective-permute-start
  67.8 164.6 %all-gather.21.cloned.1.call-start = ((), (), s32[]{:S(2)}) async-start(), calls=%async_computation.6 | async-start | bytes 1310720 | tf_op jit(solution)/shard_map/all_gather | solution.py:70
  68.6 275.1 %all-gather.13.cloned.1.call-start = ((), (), s32[]{:S(2)}) async-start(), calls=%async_computation.2 | async-start | bytes 1310720 | tf_op jit(solution)/shard_map/all_gather | solution.py:69
  99.2 1.7 copy-start.4
  232.4 3.5 copy-start.5
  236.9 14.2 %collective-permute-start.3 = (f32[512,512]{1,0:T(8,128)S(1)}, f32[512,512]{1,0:T(8,128)S(1)}, u32[]{:S(2)}, u32[]{:S(2)}) collective-permute-start(f32[512,512]{1,0:T(8,128)S(1)} %get-tuple-element.110), channel_id=1, source_target_pairs={{4,0},{8,4},{12,8},{16,12},{20,16},{24,20},{28,24},{32,28},{36,32}... | collective-permute-start | bytes 3145736 | tf_op jit(solution)/shard_map/ppermute | solution.py:12
  243.7 64.2 %collective-permute-start.2 = (f32[128,512]{0,1:T(8,128)}, f32[128,512]{0,1:T(8,128)S(1)}, u32[]{:S(2)}, u32[]{:S(2)}) collective-permute-start(f32[128,512]{0,1:T(8,128)} %fusion.103), channel_id=1, source_target_pairs={{0,4},{4,8},{8,12},{12,16},{16,20},{20,24},{24,28},{28,32},{32,36}... | collective-permute-start | bytes 786440 | tf_op jit(solution)/shard_map/ppermute | solution.py:12
  302.9 3.4 copy-start.9
  306.8 1.2 copy-start.8
  310.5 166.1 %all-gather.15.cloned.1.call-start = ((), (), s32[]{:S(2)}) async-start(), calls=%async_computation.3 | async-start | bytes 1310720 | tf_op jit(solution)/shard_map/all_gather | solution.py:70
  310.6 16.1 %collective-permute-start.4 = (f32[512,512]{1,0:T(8,128)S(1)}, f32[512,512]{1,0:T(8,128)S(1)}, u32[]{:S(2)}, u32[]{:S(2)}) collective-permute-start(f32[512,512]{1,0:T(8,128)S(1)} %pad_maximum_fusion), channel_id=1, source_target_pairs={{4,0},{8,4},{12,8},{16,12},{20,16},{24,20},{28,24},{32,28},{36,32}... | collective-permute-start | bytes 3145736 | tf_op jit(solution)/shard_map/ppermute | solution.py:12
  328.2 271.6 %all-gather.17.cloned.1.call-start = ((), (), s32[]{:S(2)}) async-start(), calls=%async_computation.4 | async-start | bytes 1310720 | tf_op jit(solution)/shard_map/all_gather | solution.py:69
  343.7 1.7 copy-start.2
  476.6 6.1 copy-start.1
  480.3 25.9 %collective-permute-start.6 = (f32[512,512]{1,0:T(8,128)S(1)}, f32[512,512]{1,0:T(8,128)S(1)}, u32[]{:S(2)}, u32[]{:S(2)}) collective-permute-start(f32[512,512]{1,0:T(8,128)S(1)} %get-tuple-element.108), channel_id=1, source_target_pairs={{8,0},{12,4},{16,8},{20,12},{24,16},{28,20},{32,24},{36,28},{40,32... | collective-permute-start | bytes 3145736 | tf_op jit(solution)/shard_map/ppermute | solution.py:12
  486.9 77.9 %collective-permute-start.5 = (f32[128,512]{0,1:T(8,128)}, f32[128,512]{0,1:T(8,128)S(1)}, u32[]{:S(2)}, u32[]{:S(2)}) collective-permute-start(f32[128,512]{0,1:T(8,128)} %fusion.101), channel_id=1, source_target_pairs={{0,8},{4,12},{8,16},{12,20},{16,24},{20,28},{24,32},{28,36},{32,40... | collective-permute-start | bytes 786440 | tf_op jit(solution)/shard_map/ppermute | solution.py:12
  558.1 4.2 copy-start.10
  562.7 2.0 copy-start.7
  567.3 165.9 %all-gather.19.cloned.1.call-start = ((), (), s32[]{:S(2)}) async-start(), calls=%async_computation.5 | async-start | bytes 1310720 | tf_op jit(solution)/shard_map/all_gather | solution.py:70
  567.4 26.0 %collective-permute-start.7 = (f32[512,512]{1,0:T(8,128)S(1)}, f32[512,512]{1,0:T(8,128)S(1)}, u32[]{:S(2)}, u32[]{:S(2)}) collective-permute-start(f32[512,512]{1,0:T(8,128)S(1)} %pad_maximum_fusion.2), channel_id=1, source_target_pairs={{8,0},{12,4},{16,8},{20,12},{24,16},{28,20},{32,24},{36,28},{40,32... | collective-permute-start | bytes 3145736 | tf_op jit(solution)/shard_map/ppermute | solution.py:12
  599.7 1.7 copy-start.3
  733.2 6.1 copy-start
  736.9 74.0 %collective-permute-start.9 = (f32[512,512]{1,0:T(8,128)S(1)}, f32[512,512]{1,0:T(8,128)S(1)}, u32[]{:S(2)}, u32[]{:S(2)}) collective-permute-start(f32[512,512]{1,0:T(8,128)S(1)} %get-tuple-element.106), channel_id=1, source_target_pairs={{16,0},{20,4},{24,8},{28,12},{32,16},{36,20},{40,24},{44,28},{48,3... | collective-permute-start | bytes 3145736 | tf_op jit(solution)/shard_map/ppermute | solution.py:12
  740.9 131.4 %collective-permute-start.10 = (f32[512,512]{1,0:T(8,128)S(1)}, f32[512,512]{1,0:T(8,128)}, u32[]{:S(2)}, u32[]{:S(2)}) collective-permute-start(f32[512,512]{1,0:T(8,128)S(1)} %pad_maximum_fusion.4), channel_id=1, source_target_pairs={{16,0},{20,4},{24,8},{28,12},{32,16},{36,20},{40,24},{44,28},{48,3... | collective-permute-start | bytes 3145736 | tf_op jit(solution)/shard_map/ppermute | solution.py:12
  745.4 124.3 %collective-permute-start.8 = (f32[128,512]{0,1:T(8,128)}, f32[128,512]{0,1:T(8,128)S(1)}, u32[]{:S(2)}, u32[]{:S(2)}) collective-permute-start(f32[128,512]{0,1:T(8,128)} %fusion.99), channel_id=1, source_target_pairs={{0,16},{4,20},{8,24},{12,28},{16,32},{20,36},{24,40},{28,44},{32,4... | collective-permute-start | bytes 786440 | tf_op jit(solution)/shard_map/ppermute | solution.py:12
  862.9 4.2 copy-start.11
  867.6 2.0 copy-start.6
Sparse Core Ops, SparseCore 0:
  22.5 41.8 all-gather.8
  67.9 31.2 all-gather.10
  101.9 32.4 all-gather.20
  310.6 33.0 all-gather.12
  346.2 30.5 all-gather.14
  567.5 32.2 all-gather.16
  602.4 30.6 all-gather.18
where the time goes:
time: 894 us; the launch traced here: 882 us
  other arithmetic  487 us (54%)
  waiting for transfers between devices  210 us (23%)
  local copies, waits for them, and re-layouts  64.4 us (7%)
  matrix products  64 us (7%)
  starting transfers between devices  32.1 us (4%)
  between operations  23.4 us (3%)
    another operation x19, other arithmetic, tri_solve(): lax.linalg.triangular_solve(factor, right, left_side=True, lower=True)  242 us
    another operation x45, other arithmetic, shards(): factor = jnp.linalg.cholesky(full_diag)  238 us
    ppermute x11, waiting for transfers between devices, passed_along(): return lax.ppermute(block, axis, route)  124 us
    another operation x79, local copies, waits for them, and re-layouts, tri_solve(): lax.linalg.triangular_solve(factor, right, left_side=True, lower=True)  55.7 us
    all_gather x3, waiting for transfers between devices, shards(): lax.all_gather(diag_rows, 'swath', axis=0, tiled=True)  50.5 us
    all_gather x1, waiting for transfers between devices, shards(): shard_rows = lax.all_gather(gram_input, 'swath', axis=0, tiled=True)  35.5 us
    another operation x42, matrix products, tri_solve(): lax.linalg.triangular_solve(factor, right, left_side=True, lower=True)  35 us
    ppermute x11, starting transfers between devices, passed_along(): return lax.ppermute(block, axis, route)  31.4 us
  transfers between devices with their start and end apart: 18, of which 11 were waited for; matrix products, arithmetic and copies ran while one was open for 66% of the time, Pallas kernels for 0%

commit v1 on v0

--- a/solution.py
+++ b/solution.py
@@ -53,7 +53,16 @@
     ahead_blocks = compact(scaled, live & (target == my_time + 1), slot_count)
     incoming, previous = passed_along((ahead_blocks, process), "tm", 1)
     gram_input = jnp.concatenate([own_blocks, incoming], axis=0).reshape(-1, order_size)
-    shard_rows = lax.all_gather(gram_input, "swath", axis=0, tiled=True)
+    shares = lax.axis_size("swath")
+    reached = sorted(((it, (it + 1) % shares) for it in range(shares)))
+    w_next = gram_input
+    chunks = [w_next]
+    for num in range(1, shares):
+        w_next = lax.ppermute(w_next, "swath", reached)
+        chunks.insert(0, w_next)
+    shard_rows = jnp.roll(
+        jnp.concatenate(chunks, 0), (lax.axis_index("swath") + 1) * gram_input.shape[0], 0
+    )
     columns = lax.dynamic_slice_in_dim(shard_rows, row_start, row_count, 1)
     gram = lax.dot_general(
         columns, shard_rows, (((0,), (0,)), ((), ())), preferred_element_type=jnp.float32

time: 894 us -> 837 us (0.936)
  the two profiles are of different devices: /device:TPU:16 before, /device:TPU:48 now
where the time goes in v1:
time: 837 us; the launch traced here: 832 us
  other arithmetic  496 us (59%)
  waiting for transfers between devices  129 us (15%)
  matrix products  75.9 us (9%)
  local copies, waits for them, and re-layouts  65.3 us (8%)
  starting transfers between devices  42.5 us (5%)
  between operations  23.6 us (3%)
    another operation x19, other arithmetic, tri_solve(): lax.linalg.triangular_solve(factor, right, left_side=True, lower=True)  248 us
    another operation x45, other arithmetic, shards(): factor = jnp.linalg.cholesky(full_diag)  238 us
    another operation x79, local copies, waits for them, and re-layouts, tri_solve(): lax.linalg.triangular_solve(factor, right, left_side=True, lower=True)  56.5 us
    all_gather x3, waiting for transfers between devices, shards(): lax.all_gather(diag_rows, 'swath', axis=0, tiled=True)  55.8 us
    another operation x42, matrix products, tri_solve(): lax.linalg.triangular_solve(factor, right, left_side=True, lower=True)  45.5 us
    ppermute x11, waiting for transfers between devices, passed_along(): return lax.ppermute(block, axis, route)  39.5 us
    ppermute x11, starting transfers between devices, passed_along(): return lax.ppermute(block, axis, route)  34.2 us
    ppermute x3, waiting for transfers between devices, shards(): w_next = lax.ppermute(w_next, 'swath', reached)  33.3 us
  transfers between devices with their start and end apart: 20, of which 9 were waited for; matrix products, arithmetic and copies ran while one was open for 74% of the time, Pallas kernels for 0%

profile of v1, /device:TPU:48, one launch (start us, length us, event | category | flops | bytes accessed | tf_op | source)
XLA Modules:
  0.0 832.0 jit_solution(7356956746891819887)
XLA Ops:
  17.1 4.4 collective-permute-done.1
  21.6 3.4 collective-permute-start.2
  25.0 11.8 %collective-permute-done.2 = bf16[512,512]{1,0:T(8,128)(2,1)S(1)} collective-permute-done((bf16[512,512]{1,0:T(8,128)(2,1)S(1)}, bf16[512,512]{1,0:T(8,128)(2,1)S(1)}, u32[]{:S(2)}, u32[]{:S(2)}) %collective-permute-start.2) | collective-permute-done | bytes 524320 | tf_op jit(solution)/shard_map/ppermute | solution.py:61
  39.0 12.1 %collective-permute-done.3 = bf16[512,512]{1,0:T(8,128)(2,1)S(1)} collective-permute-done((bf16[512,512]{1,0:T(8,128)(2,1)S(1)}, bf16[512,512]{1,0:T(8,128)(2,1)S(1)}, u32[]{:S(2)}, u32[]{:S(2)}) %collective-permute-start.3) | collective-permute-done | bytes 524320 | tf_op jit(solution)/shard_map/ppermute | solution.py:61
  55.2 9.4 %collective-permute-done.4 = bf16[512,512]{1,0:T(8,128)(2,1)S(1)} collective-permute-done((bf16[512,512]{1,0:T(8,128)(2,1)S(1)}, bf16[512,512]{1,0:T(8,128)(2,1)S(1)}, u32[]{:S(2)}, u32[]{:S(2)}) %collective-permute-start.4) | collective-permute-done | bytes 524320 | tf_op jit(solution)/shard_map/ppermute | solution.py:61
  68.2 36.1 %all-gather.8.cloned.1.call-done = f32[512,512]{0,1:T(8,128)} async-done(((f32[128,512]{0,1:T(8,128)}), f32[512,512]{0,1:T(8,128)}) %all-gather.8.cloned.1.call-update) | async-done | bytes 1048592 | tf_op jit(solution)/shard_map/all_gather | solution.py:78
  107.3 11.7 %cholesky.374 = f32[128,128]{1,0:T(8,128)S(1)} custom-call(f32[128,128]{1,0:T(8,128)S(1)} %cholesky.586), custom_call_target="Cholesky" | custom-call | tf_op jit(solution)/shard_map/jit(cholesky)/cholesky | solution.py:81
  119.2 9.8 %custom-call.34 = f32[1,128,128]{1,2,0:T(8,128)S(1)} custom-call(f32[1,128,128]{2,1,0:T(8,128)S(1)} %get-tuple-element.152), custom_call_target="InvertDiagBlocksLowerTriangular" | custom-call | tf_op jit(solution)/shard_map/jit(cholesky)/cholesky | solution.py:81
  129.6 11.7 %cholesky.393 = f32[128,128]{1,0:T(8,128)S(1)} custom-call(f32[128,128]{1,0:T(8,128)S(1)} %cholesky.590), custom_call_target="Cholesky" | custom-call | tf_op jit(solution)/shard_map/jit(cholesky)/cholesky | solution.py:81
  142.7 10.0 %custom-call.35 = f32[1,128,128]{1,2,0:T(8,128)S(1)} custom-call(f32[1,128,128]{2,1,0:T(8,128)S(1)} %get-tuple-element.149), custom_call_target="InvertDiagBlocksLowerTriangular" | custom-call | tf_op jit(solution)/shard_map/jit(cholesky)/cholesky | solution.py:81
  153.3 11.7 %cholesky.414 = f32[128,128]{1,0:T(8,128)S(1)} custom-call(f32[128,128]{1,0:T(8,128)S(1)} %cholesky.595), custom_call_target="Cholesky" | custom-call | tf_op jit(solution)/shard_map/jit(cholesky)/cholesky | solution.py:81
  165.7 9.8 %custom-call.36 = f32[1,128,128]{1,2,0:T(8,128)S(1)} custom-call(f32[1,128,128]{2,1,0:T(8,128)S(1)} %get-tuple-element.146), custom_call_target="InvertDiagBlocksLowerTriangular" | custom-call | tf_op jit(solution)/shard_map/jit(cholesky)/cholesky | solution.py:81
  176.1 11.7 %cholesky.431 = f32[128,128]{1,0:T(8,128)S(1)} custom-call(f32[128,128]{1,0:T(8,128)S(1)} %convolution_subtract_fusion.14), custom_call_target="Cholesky" | custom-call | tf_op jit(solution)/shard_map/jit(cholesky)/cholesky | solution.py:81
  193.6 7.9 while.12
  201.4 39.3 %custom-call.37 = f32[4,128,128]{1,2,0:T(8,128)S(1)} custom-call(f32[4,128,128]{2,1,0:T(8,128)S(1)} %get-tuple-element.47), custom_call_target="InvertDiagBlocksLowerTriangular" | custom-call | tf_op jit(solution)/shard_map/triangular_solve/custom-call.3 | solution.py:16
  256.6 10.4 %while.13 = (s32[]{:T(128)}, f32[512,512]{1,0:T(8,128)S(1)}, s32[4,2]{0,1:T(2,128)S(1)}, f32[4,128,128]{2,1,0:T(8,128)}, s32[]{:T(128)}) while((s32[]{:T(128)}, f32[512,512]{1,0:T(8,128)S(1)}, s32[4,2]{0,1:T(2,128)S(1)}, f32[4,128,128]{2,1,0:T(8,128)}, s32[]{:T(128)}) %tuple.155), condition=%wide.while_cond.clone, body=%wide.while_body.clone.sunk | while | flops 2 | bytes 132705 | solution.py:16
  267.0 40.8 %custom-call.38 = f32[4,128,128]{1,2,0:T(8,128)} custom-call(f32[4,128,128]{2,1,0:T(8,128)} %get-tuple-element.48), custom_call_target="InvertDiagBlocksLowerTriangular" | custom-call | tf_op jit(solution)/shard_map/triangular_solve/custom-call.3 | solution.py:16
  314.4 3.5 subtract_subtract_fusion.1
  321.1 12.3 %collective-permute-done.7 = f32[512,512]{1,0:T(8,128)S(1)} collective-permute-done((f32[512,512]{1,0:T(8,128)S(1)}, f32[512,512]{1,0:T(8,128)S(1)}, u32[]{:S(2)}, u32[]{:S(2)}) %collective-permute-start.7) | collective-permute-done | bytes 1048608 | tf_op jit(solution)/shard_map/ppermute | solution.py:12
  335.1 15.2 %all-gather.10.cloned.1.call-done = f32[512,512]{0,1:T(8,128)} async-done(((f32[128,512]{0,1:T(8,128)}), f32[512,512]{0,1:T(8,128)}) %all-gather.10.cloned.1.call-update) | async-done | bytes 1048592 | tf_op jit(solution)/shard_map/all_gather | solution.py:78
  353.3 11.7 %cholesky.446 = f32[128,128]{1,0:T(8,128)S(1)} custom-call(f32[128,128]{1,0:T(8,128)S(1)} %cholesky.599), custom_call_target="Cholesky" | custom-call | tf_op jit(solution)/shard_map/jit(cholesky)/cholesky | solution.py:81
  365.2 9.8 %custom-call.39 = f32[1,128,128]{1,2,0:T(8,128)S(1)} custom-call(f32[1,128,128]{2,1,0:T(8,128)S(1)} %get-tuple-element.142), custom_call_target="InvertDiagBlocksLowerTriangular" | custom-call | tf_op jit(solution)/shard_map/jit(cholesky)/cholesky | solution.py:81
  375.7 11.7 %cholesky.465 = f32[128,128]{1,0:T(8,128)S(1)} custom-call(f32[128,128]{1,0:T(8,128)S(1)} %cholesky.603), custom_call_target="Cholesky" | custom-call | tf_op jit(solution)/shard_map/jit(cholesky)/cholesky | solution.py:81
  388.7 10.0 %custom-call.40 = f32[1,128,128]{1,2,0:T(8,128)S(1)} custom-call(f32[1,128,128]{2,1,0:T(8,128)S(1)} %get-tuple-element.139), custom_call_target="InvertDiagBlocksLowerTriangular" | custom-call | tf_op jit(solution)/shard_map/jit(cholesky)/cholesky | solution.py:81
  399.4 11.7 %cholesky.486 = f32[128,128]{1,0:T(8,128)S(1)} custom-call(f32[128,128]{1,0:T(8,128)S(1)} %cholesky.608), custom_call_target="Cholesky" | custom-call | tf_op jit(solution)/shard_map/jit(cholesky)/cholesky | solution.py:81
  411.8 9.8 %custom-call.41 = f32[1,128,128]{1,2,0:T(8,128)S(1)} custom-call(f32[1,128,128]{2,1,0:T(8,128)S(1)} %get-tuple-element.136), custom_call_target="InvertDiagBlocksLowerTriangular" | custom-call | tf_op jit(solution)/shard_map/jit(cholesky)/cholesky | solution.py:81
  422.2 11.7 %cholesky.503 = f32[128,128]{1,0:T(8,128)S(1)} custom-call(f32[128,128]{1,0:T(8,128)S(1)} %convolution_subtract_fusion.13), custom_call_target="Cholesky" | custom-call | tf_op jit(solution)/shard_map/jit(cholesky)/cholesky | solution.py:81
  441.0 7.9 while.14
  448.9 39.9 %custom-call.42 = f32[4,128,128]{1,2,0:T(8,128)} custom-call(f32[4,128,128]{2,1,0:T(8,128)S(1)} %get-tuple-element.49), custom_call_target="InvertDiagBlocksLowerTriangular" | custom-call | tf_op jit(solution)/shard_map/triangular_solve/custom-call.3 | solution.py:16
  503.3 10.6 %while.15 = (s32[]{:T(128)}, f32[512,512]{1,0:T(8,128)S(1)}, s32[4,2]{0,1:T(2,128)S(1)}, f32[4,128,128]{2,1,0:T(8,128)}, s32[]{:T(128)}) while((s32[]{:T(128)}, f32[512,512]{1,0:T(8,128)S(1)}, s32[4,2]{0,1:T(2,128)S(1)}, f32[4,128,128]{2,1,0:T(8,128)}, s32[]{:T(128)}) %tuple.157), condition=%wide.while_cond.clone.2, body=%wide.while_body.clone.2.sunk | while | flops 2 | bytes 132705 | solution.py:16
  513.9 40.8 %custom-call.43 = f32[4,128,128]{1,2,0:T(8,128)} custom-call(f32[4,128,128]{2,1,0:T(8,128)} %get-tuple-element.50), custom_call_target="InvertDiagBlocksLowerTriangular" | custom-call | tf_op jit(solution)/shard_map/triangular_solve/custom-call.3 | solution.py:16
  563.0 3.5 subtract_subtract_fusion
  566.5 3.6 collective-permute-start.10
  570.1 22.8 %collective-permute-done.10 = f32[512,512]{1,0:T(8,128)S(1)} collective-permute-done((f32[512,512]{1,0:T(8,128)S(1)}, f32[512,512]{1,0:T(8,128)S(1)}, u32[]{:S(2)}, u32[]{:S(2)}) %collective-permute-start.10) | collective-permute-done | bytes 1048608 | tf_op jit(solution)/shard_map/ppermute | solution.py:12
  594.4 4.5 all-gather.14.cloned.1.call-done
  601.9 11.7 %cholesky.518 = f32[128,128]{1,0:T(8,128)S(1)} custom-call(f32[128,128]{1,0:T(8,128)S(1)} %cholesky.612), custom_call_target="Cholesky" | custom-call | tf_op jit(solution)/shard_map/jit(cholesky)/cholesky | solution.py:81
  613.8 9.8 %custom-call.44 = f32[1,128,128]{1,2,0:T(8,128)S(1)} custom-call(f32[1,128,128]{2,1,0:T(8,128)S(1)} %get-tuple-element.132), custom_call_target="InvertDiagBlocksLowerTriangular" | custom-call | tf_op jit(solution)/shard_map/jit(cholesky)/cholesky | solution.py:81
  624.3 11.7 %cholesky.537 = f32[128,128]{1,0:T(8,128)S(1)} custom-call(f32[128,128]{1,0:T(8,128)S(1)} %cholesky.616), custom_call_target="Cholesky" | custom-call | tf_op jit(solution)/shard_map/jit(cholesky)/cholesky | solution.py:81
  637.4 10.2 %custom-call.45 = f32[1,128,128]{1,2,0:T(8,128)S(1)} custom-call(f32[1,128,128]{2,1,0:T(8,128)S(1)} %get-tuple-element.129), custom_call_target="InvertDiagBlocksLowerTriangular" | custom-call | tf_op jit(solution)/shard_map/jit(cholesky)/cholesky | solution.py:81
  648.2 11.7 %cholesky.558 = f32[128,128]{1,0:T(8,128)S(1)} custom-call(f32[128,128]{1,0:T(8,128)S(1)} %cholesky.621), custom_call_target="Cholesky" | custom-call | tf_op jit(solution)/shard_map/jit(cholesky)/cholesky | solution.py:81
  660.7 9.8 %custom-call.46 = f32[1,128,128]{1,2,0:T(8,128)S(1)} custom-call(f32[1,128,128]{2,1,0:T(8,128)S(1)} %get-tuple-element.126), custom_call_target="InvertDiagBlocksLowerTriangular" | custom-call | tf_op jit(solution)/shard_map/jit(cholesky)/cholesky | solution.py:81
  671.1 11.9 %cholesky.575 = f32[128,128]{1,0:T(8,128)S(1)} custom-call(f32[128,128]{1,0:T(8,128)S(1)} %convolution_subtract_fusion.12), custom_call_target="Cholesky" | custom-call | tf_op jit(solution)/shard_map/jit(cholesky)/cholesky | solution.py:81
  686.5 4.2 collective-permute-start.12
  690.7 7.8 while.16
  698.6 39.9 %custom-call.47 = f32[4,128,128]{1,2,0:T(8,128)} custom-call(f32[4,128,128]{2,1,0:T(8,128)S(1)} %get-tuple-element.51), custom_call_target="InvertDiagBlocksLowerTriangular" | custom-call | tf_op jit(solution)/shard_map/triangular_solve/custom-call.3 | solution.py:16
  750.6 6.6 collective-permute-start.11
  759.4 10.1 %while.17 = (s32[]{:T(128)}, f32[512,512]{1,0:T(8,128)S(1)}, s32[4,2]{0,1:T(2,128)S(1)}, f32[4,128,128]{2,1,0:T(8,128)}, s32[]{:T(128)}) while((s32[]{:T(128)}, f32[512,512]{1,0:T(8,128)S(1)}, s32[4,2]{0,1:T(2,128)S(1)}, f32[4,128,128]{2,1,0:T(8,128)}, s32[]{:T(128)}) %tuple.159), condition=%wide.while_cond.clone.4, body=%wide.while_body.clone.4.sunk | while | flops 2 | bytes 132705 | solution.py:16
  769.5 40.8 %custom-call.48 = f32[4,128,128]{1,2,0:T(8,128)} custom-call(f32[4,128,128]{2,1,0:T(8,128)} %get-tuple-element.52), custom_call_target="InvertDiagBlocksLowerTriangular" | custom-call | tf_op jit(solution)/shard_map/triangular_solve/custom-call.3 | solution.py:16
  (283 shorter events, 183.6 us)
Async XLA Ops:
  7.2 45.9 %copy-start.6 = (bf16[1,128,512]{2,1,0:T(8,128)(2,1)S(1)}, bf16[1,128,512]{2,1,0:T(8,128)(2,1)}, u32[]{:S(2)}) copy-start(bf16[1,128,512]{2,1,0:T(8,128)(2,1)} %param.11) | copy-start | bytes 393220
  7.2 97.1 %all-gather.8.cloned.1.call-start = ((), (), s32[]{:S(2)}) async-start(), calls=%async_computation | async-start | bytes 1310720 | tf_op jit(solution)/shard_map/all_gather | solution.py:78
  13.9 7.7 collective-permute-start.1
  21.6 15.2 %collective-permute-start.2 = (bf16[512,512]{1,0:T(8,128)(2,1)S(1)}, bf16[512,512]{1,0:T(8,128)(2,1)S(1)}, u32[]{:S(2)}, u32[]{:S(2)}) collective-permute-start(bf16[512,512]{1,0:T(8,128)(2,1)S(1)} %bitcast.250), channel_id=1, source_target_pairs={{0,1},{1,2},{2,3},{3,0},{4,5},{5,6},{6,7},{7,4},{8,9},{9,10},{10,1... | collective-permute-start | bytes 1572872 | tf_op jit(solution)/shard_map/ppermute | solution.py:61
  36.9 14.3 %collective-permute-start.3 = (bf16[512,512]{1,0:T(8,128)(2,1)S(1)}, bf16[512,512]{1,0:T(8,128)(2,1)S(1)}, u32[]{:S(2)}, u32[]{:S(2)}) collective-permute-start(bf16[512,512]{1,0:T(8,128)(2,1)S(1)} %collective-permute-done.2), channel_id=1, source_target_pairs={{0,1},{1,2},{2,3},{3,0},{4,5},{5,6},{6,7},{7,4},{8,9},{9,10},{10,1... | collective-permute-start | bytes 1572872 | tf_op jit(solution)/shard_map/ppermute | solution.py:61
  51.2 13.4 %collective-permute-start.4 = (bf16[512,512]{1,0:T(8,128)(2,1)S(1)}, bf16[512,512]{1,0:T(8,128)(2,1)S(1)}, u32[]{:S(2)}, u32[]{:S(2)}) collective-permute-start(bf16[512,512]{1,0:T(8,128)(2,1)S(1)} %collective-permute-done.3), channel_id=1, source_target_pairs={{0,1},{1,2},{2,3},{3,0},{4,5},{5,6},{6,7},{7,4},{8,9},{9,10},{10,1... | collective-permute-start | bytes 1572872 | tf_op jit(solution)/shard_map/ppermute | solution.py:61
  53.2 11.7 %collective-permute-start = (bf16[1,128,512]{1,2,0:T(8,128)(2,1)S(1)}, bf16[1,128,512]{1,2,0:T(8,128)(2,1)S(1)}, u32[]{:S(2)}, u32[]{:S(2)}) collective-permute-start(bf16[1,128,512]{1,2,0:T(8,128)(2,1)S(1)} %copy.20), channel_id=1, source_target_pairs={{0,4},{4,8},{8,12},{12,16},{16,20},{20,24},{24,28},{28,32},{32,36}... | collective-permute-start | bytes 393224 | tf_op jit(solution)/shard_map/ppermute | solution.py:12
  55.2 9.7 %copy-start.7 = (f32[1,128]{1,0:T(1,128)S(1)}, f32[1,128]{1,0:T(1,128)}, u32[]{:S(2)}) copy-start(f32[1,128]{1,0:T(1,128)} %param.12) | copy-start | bytes 1540
  66.8 173.9 %all-gather.18.cloned.1.call-start = ((), (), s32[]{:S(2)}) async-start(), calls=%async_computation.5 | async-start | bytes 1310720 | tf_op jit(solution)/shard_map/all_gather | solution.py:79
  67.6 282.6 %all-gather.10.cloned.1.call-start = ((), (), s32[]{:S(2)}) async-start(), calls=%async_computation.1 | async-start | bytes 1310720 | tf_op jit(solution)/shard_map/all_gather | solution.py:78
  191.6 62.9 %collective-permute-start.6 = (f32[512,512]{1,0:T(8,128)S(1)}, f32[512,512]{1,0:T(8,128)}, u32[]{:S(2)}, u32[]{:S(2)}) collective-permute-start(f32[512,512]{1,0:T(8,128)S(1)} %get-tuple-element.110), channel_id=1, source_target_pairs={{4,0},{8,4},{12,8},{16,12},{20,16},{24,20},{28,24},{32,28},{36,32}... | collective-permute-start | bytes 3145736 | tf_op jit(solution)/shard_map/ppermute | solution.py:12
  246.5 61.2 %copy-start.2 = (f32[1,512,512]{1,2,0:T(8,128)S(1)}, f32[1,512,512]{1,2,0:T(8,128)}, u32[]{:S(2)}) copy-start(f32[1,512,512]{1,2,0:T(8,128)} %all-gather.18.cloned.1.call-done) | copy-start | bytes 3145732
  252.1 62.3 %collective-permute-start.5 = (f32[128,512]{0,1:T(8,128)}, f32[128,512]{0,1:T(8,128)}, u32[]{:S(2)}, u32[]{:S(2)}) collective-permute-start(f32[128,512]{0,1:T(8,128)} %fusion.104), channel_id=1, source_target_pairs={{0,4},{4,8},{8,12},{12,16},{16,20},{20,24},{24,28},{28,32},{32,36}... | collective-permute-start | bytes 786440 | tf_op jit(solution)/shard_map/ppermute | solution.py:12
  267.0 47.4 %copy-start.5 = (f32[128,512]{0,1:T(8,128)S(1)}, f32[128,512]{0,1:T(8,128)}, u32[]{:S(2)}) copy-start(f32[128,512]{0,1:T(8,128)} %fusion.72) | copy-start | bytes 786436
  317.9 171.0 %all-gather.12.cloned.1.call-start = ((), (), s32[]{:S(2)}) async-start(), calls=%async_computation.2 | async-start | bytes 1310720 | tf_op jit(solution)/shard_map/all_gather | solution.py:79
  317.9 15.5 %collective-permute-start.7 = (f32[512,512]{1,0:T(8,128)S(1)}, f32[512,512]{1,0:T(8,128)S(1)}, u32[]{:S(2)}, u32[]{:S(2)}) collective-permute-start(f32[512,512]{1,0:T(8,128)S(1)} %pad_maximum_fusion), channel_id=1, source_target_pairs={{4,0},{8,4},{12,8},{16,12},{20,16},{24,20},{28,24},{32,28},{36,32}... | collective-permute-start | bytes 3145736 | tf_op jit(solution)/shard_map/ppermute | solution.py:12
  334.9 264.0 %all-gather.14.cloned.1.call-start = ((), (), s32[]{:S(2)}) async-start(), calls=%async_computation.3 | async-start | bytes 1310720 | tf_op jit(solution)/shard_map/all_gather | solution.py:78
  437.7 63.5 %collective-permute-start.9 = (f32[512,512]{1,0:T(8,128)S(1)}, f32[512,512]{1,0:T(8,128)}, u32[]{:S(2)}, u32[]{:S(2)}) collective-permute-start(f32[512,512]{1,0:T(8,128)S(1)} %get-tuple-element.108), channel_id=1, source_target_pairs={{8,0},{12,4},{16,8},{20,12},{24,16},{28,20},{32,24},{36,28},{40,32... | collective-permute-start | bytes 3145736 | tf_op jit(solution)/shard_map/ppermute | solution.py:12
  488.8 5.8 copy-start.1
  498.5 64.5 %collective-permute-start.8 = (f32[128,512]{0,1:T(8,128)}, f32[128,512]{0,1:T(8,128)}, u32[]{:S(2)}, u32[]{:S(2)}) collective-permute-start(f32[128,512]{0,1:T(8,128)} %fusion.102), channel_id=1, source_target_pairs={{0,8},{4,12},{8,16},{12,20},{16,24},{20,28},{24,32},{28,36},{32,40... | collective-permute-start | bytes 786440 | tf_op jit(solution)/shard_map/ppermute | solution.py:12
  513.9 49.1 %copy-start.4 = (f32[128,512]{0,1:T(8,128)S(1)}, f32[128,512]{0,1:T(8,128)}, u32[]{:S(2)}) copy-start(f32[128,512]{0,1:T(8,128)} %subtract_subtract_fusion.1) | copy-start | bytes 786436
  566.5 172.0 %all-gather.16.cloned.1.call-start = ((), (), s32[]{:S(2)}) async-start(), calls=%async_computation.4 | async-start | bytes 1310720 | tf_op jit(solution)/shard_map/all_gather | solution.py:79
  566.5 26.3 %collective-permute-start.10 = (f32[512,512]{1,0:T(8,128)S(1)}, f32[512,512]{1,0:T(8,128)S(1)}, u32[]{:S(2)}, u32[]{:S(2)}) collective-permute-start(f32[512,512]{1,0:T(8,128)S(1)} %pad_maximum_fusion.2), channel_id=1, source_target_pairs={{8,0},{12,4},{16,8},{20,12},{24,16},{28,20},{32,24},{36,28},{40,32... | collective-permute-start | bytes 3145736 | tf_op jit(solution)/shard_map/ppermute | solution.py:12
  686.5 70.8 %collective-permute-start.12 = (f32[512,512]{1,0:T(8,128)S(1)}, f32[512,512]{1,0:T(8,128)}, u32[]{:S(2)}, u32[]{:S(2)}) collective-permute-start(f32[512,512]{1,0:T(8,128)S(1)} %get-tuple-element.106), channel_id=1, source_target_pairs={{16,0},{20,4},{24,8},{28,12},{32,16},{36,20},{40,24},{44,28},{48,3... | collective-permute-start | bytes 3145736 | tf_op jit(solution)/shard_map/ppermute | solution.py:12
  738.5 5.8 copy-start
  745.7 76.5 %collective-permute-start.13 = (f32[512,512]{1,0:T(8,128)S(1)}, f32[512,512]{1,0:T(8,128)}, u32[]{:S(2)}, u32[]{:S(2)}) collective-permute-start(f32[512,512]{1,0:T(8,128)S(1)} %pad_maximum_fusion.4), channel_id=1, source_target_pairs={{16,0},{20,4},{24,8},{28,12},{32,16},{36,20},{40,24},{44,28},{48,3... | collective-permute-start | bytes 3145736 | tf_op jit(solution)/shard_map/ppermute | solution.py:12
  750.6 67.9 %collective-permute-start.11 = (f32[128,512]{0,1:T(8,128)}, f32[128,512]{0,1:T(8,128)}, u32[]{:S(2)}, u32[]{:S(2)}) collective-permute-start(f32[128,512]{0,1:T(8,128)} %fusion.100), channel_id=1, source_target_pairs={{0,16},{4,20},{8,24},{12,28},{16,32},{20,36},{24,40},{28,44},{32,4... | collective-permute-start | bytes 786440 | tf_op jit(solution)/shard_map/ppermute | solution.py:12
  769.5 49.1 %copy-start.3 = (f32[128,512]{0,1:T(8,128)S(1)}, f32[128,512]{0,1:T(8,128)}, u32[]{:S(2)}) copy-start(f32[128,512]{0,1:T(8,128)} %subtract_subtract_fusion) | copy-start | bytes 786436
Sparse Core Ops, SparseCore 0:
  67.0 37.2 all-gather.7
  106.9 31.9 all-gather.17
  318.0 32.2 all-gather.9
  352.8 30.7 all-gather.11
  566.6 32.2 all-gather.13
  601.4 30.7 all-gather.15
